TPU v7x, 256 devices: a whole 4x4x8 slice. The times are simulated.
256 devices in a mesh: tm: 32 (over y, x, core), space: 8 (over z).
Axes of the slice: x: 4, y: 4, z: 8, core: 2. Of those that a mesh axis runs over, the one named last changes fastest.
Arguments:
- point_states: float32 [32, 256, 1024], P('tm', 'space'), may hold values from -6 to 6
- initial_state: float32 [256, 1024], P('space'), may hold values from -6 to 6
- node_rate: float32 [256, 1024], P('space'), may hold values from 0.01 to 0.06
- source_map: float32 [256, 1024], P('space'), may hold values from -6 to 6
- waveform: float32 [512], replicated, may hold values from -2 to 2
- cond_table: float32 [16], replicated, may hold values from 0.25 to 4
- class_map: int32 [32, 8], P('space'), may hold values from 0 to 15
- interval_steps: int32 [32], replicated, may hold values from 1 to 20, 512 in all
Outputs:
- corrected: float32 [32, 256, 1024], P('tm', 'space')
Inputs may be any that keep to these rules, and one draw needn't show every extreme that they name: `interval_steps`: they sum to 512 and the largest equals 20.
All inputs are finite; a program needn't handle non-finite values.
Results may differ from a plain program's by a relative error of at most 0.0003.
Values sent between devices are 32-bit elements; how exact they have to be, the bound alone decides.
A program may use at most 64 MiB of HBM per device.

v0:
```python
import jax
import jax.numpy as jnp
from jax import lax
from jax.sharding import PartitionSpec as P

STEP_MOST = 20
CSUB = 5
BLK_R = 8
BLK_C = 128


def with_halo(shard, sides, width):
    for axis, dim in sides:
        peers, length = (lax.axis_size(axis), shard.shape[dim])
        up = [(i, (i + 1) % peers) for i in range(peers - 1)]
        down = [(j, i) for i, j in up]
        last = lax.slice_in_dim(shard, length - width, length, axis=dim)
        first = lax.slice_in_dim(shard, 0, width, axis=dim)
        before = lax.ppermute(last, axis, up)
        after = lax.ppermute(first, axis, down)
        shard = jnp.concatenate([before, shard, after], axis=dim)
    return shard


def passed_along(value, axis, steps):
    count = lax.axis_size(axis)
    first, last = (max(0, -steps), min(count, count - steps))
    return lax.ppermute(value, axis, [(source, source + steps) for source in range(first, last)])


def neighbours(values):
    zero_row = jnp.zeros_like(values[..., :1, :])
    zero_col = jnp.zeros_like(values[..., :, :1])
    above_row = jnp.concatenate([zero_row, values[..., :-1, :]], axis=-2)
    below_row = jnp.concatenate([values[..., 1:, :], zero_row], axis=-2)
    left_col = jnp.concatenate([zero_col, values[..., :, :-1]], axis=-1)
    right_col = jnp.concatenate([values[..., :, 1:], zero_col], axis=-1)
    return (above_row, below_row, left_col, right_col)


def side_cols(values):
    zero_col = jnp.zeros_like(values[..., :, :1])
    left_col = jnp.concatenate([zero_col, values[..., :, :-1]], axis=-1)
    right_col = jnp.concatenate([values[..., :, 1:], zero_col], axis=-1)
    return (left_col, right_col)


def restrict(values):
    return 0.25 * (
        values[..., 0::2, 0::2]
        + values[..., 1::2, 0::2]
        + (values[..., 0::2, 1::2] + values[..., 1::2, 1::2])
    )


def prolong(values):
    return jnp.repeat(jnp.repeat(values, 2, axis=-2), 2, axis=-1)


def node_conductance(class_map, cond_table):
    classes = jnp.arange(cond_table.shape[0], dtype=jnp.int32)
    picked = jnp.sum(
        jnp.where(class_map[None] == classes[:, None, None], cond_table[:, None, None], 0.0), axis=0
    )
    return jnp.repeat(jnp.repeat(picked, BLK_R, axis=0), BLK_C, axis=1)


def base_weights(rates, conduct):
    above_row, below_row, left_col, right_col = neighbours(conduct)
    return (
        rates * jnp.sqrt(conduct * above_row),
        rates * jnp.sqrt(conduct * below_row),
        rates * jnp.sqrt(conduct * left_col),
        rates * jnp.sqrt(conduct * right_col),
    )


def combine(state_now, above_row, below_row, left_col, right_col, weights, forcing):
    to_above, to_below, to_left, to_right = weights
    return (
        state_now
        + (
            to_above * (above_row - state_now)
            + to_below * (below_row - state_now)
            + to_left * (left_col - state_now)
            + to_right * (right_col - state_now)
        )
        + forcing
    )


def coarse_step(carried, coarse_weights, factor):
    to_above, to_below, to_left, to_right = coarse_weights
    above_row, below_row, left_col, right_col = neighbours(carried)
    return carried + factor * (
        to_above * (above_row - carried)
        + to_below * (below_row - carried)
        + to_left * (left_col - carried)
        + to_right * (right_col - carried)
    )


def run_block(incoming, residues, coarse_weights, factors, trim):
    carried = incoming
    error_list = [carried]
    for substep in range(CSUB):
        carried = coarse_step(carried, coarse_weights, factors[0])
    carried = carried + residues[0]
    errors = jnp.stack(error_list)
    return (carried[trim:-trim], errors[:, trim:-trim])


def shards(
    point_states,
    initial_state,
    node_rate,
    source_map,
    waveform,
    cond_table,
    class_map,
    interval_steps,
):
    per_dev = point_states.shape[0]
    my_index = lax.axis_index("tm")
    conduct = node_conductance(class_map, cond_table)
    conduct_rim = with_halo(conduct, (("space", 0),), 1)
    left_g, right_g = side_cols(conduct)
    weights = (
        node_rate * jnp.sqrt(conduct * conduct_rim[:-2]),
        node_rate * jnp.sqrt(conduct * conduct_rim[2:]),
        node_rate * jnp.sqrt(conduct * left_g),
        node_rate * jnp.sqrt(conduct * right_g),
    )
    starts_all = jnp.cumsum(interval_steps) - interval_steps
    my_starts = lax.dynamic_slice_in_dim(starts_all, my_index * per_dev, per_dev)
    counts = lax.dynamic_slice_in_dim(interval_steps, my_index * per_dev, per_dev)
    positions = jnp.arange(waveform.shape[0], dtype=jnp.int32)

    def wave_at(fine_step):
        hits = positions[None, :] == (my_starts + fine_step)[:, None]
        return jnp.sum(jnp.where(hits, waveform[None, :], 0.0), axis=1)

    def sweep(state_in):
        state_now = state_in
        for fine_step in range(STEP_MOST):
            padded = with_halo(state_now, (("space", 1),), 1)
            left_col, right_col = side_cols(state_now)
            forcing = wave_at(fine_step)[:, None, None] * source_map
            updated = combine(
                state_now, padded[:, :-2], padded[:, 2:], left_col, right_col, weights, forcing
            )
            state_now = jnp.where((fine_step < counts)[:, None, None], updated, state_now)
        return state_now

    first_pass = sweep(point_states)
    incoming = passed_along(first_pass[-1], "tm", 1)
    head_state = jnp.where(my_index == 0, initial_state, incoming)
    relaxed = jnp.concatenate([head_state[None], first_pass[:-1]], axis=0)
    second_pass = sweep(relaxed)
    change = restrict(second_pass - first_pass)
    factors = counts.astype(jnp.float32) / (4.0 * CSUB)
    rim_width = per_dev * CSUB
    stacked = jnp.concatenate([change, restrict(node_rate)[None], restrict(conduct)[None]], axis=0)
    widened = with_halo(stacked, (("space", 1),), rim_width + 1)
    full_weights = base_weights(widened[per_dev], widened[per_dev + 1])
    coarse_weights = (
        full_weights[0][1:-1],
        full_weights[1][1:-1],
        full_weights[2][1:-1],
        full_weights[3][1:-1],
    )
    residues = widened[:per_dev, 1:-1]

    def one_turn(turn_index, carry):
        outgoing, stored = carry
        received = passed_along(outgoing, "tm", 1)
        beside_all = with_halo(received, (("space", 0),), rim_width)
        return lax.cond(
            turn_index == my_index,
            lambda: run_block(beside_all, residues, coarse_weights, factors, rim_width),
            lambda: (outgoing, stored),
        )

    start_carry = (jnp.zeros_like(change[0]), jnp.zeros_like(change))
    unused, errors = lax.fori_loop(0, lax.axis_size("tm"), one_turn, start_carry)
    return relaxed + prolong(errors)


def solution(mesh):
    placed = (
        P("tm", "space", None),
        P("space", None),
        P("space", None),
        P("space", None),
        P(),
        P(),
        P("space", None),
        P(),
    )
    return jax.shard_map(
        shards, mesh=mesh, in_specs=placed, out_specs=P("tm", "space", None), check_vma=False
    )
```

profile of v0, /device:TPU:136, one launch (start us, length us, event | category | flops | bytes accessed | tf_op | source)
XLA Modules:
  0.0 972.6 jit_solution(9197214484908586694)
XLA Ops:
  66.1 5.4 collective-permute-start.10
  90.0 5.4 collective-permute-start.14
  99.4 5.4 collective-permute-start.16
  108.8 5.4 collective-permute-start.18
  118.2 5.6 collective-permute-start.20
  127.7 5.4 collective-permute-start.22
  137.0 5.4 collective-permute-start.24
  146.4 5.4 collective-permute-start.26
  155.8 5.4 collective-permute-start.28
  174.6 5.4 collective-permute-start.32
  184.0 5.4 collective-permute-start.34
  193.4 5.4 collective-permute-start.36
  212.3 5.4 collective-permute-start.40
  231.3 5.4 collective-permute-start.44
  240.8 6.4 collective-permute-done.45
  258.6 5.4 collective-permute-start.49
  268.0 5.4 collective-permute-start.51
  277.4 5.4 collective-permute-start.53
  286.8 5.4 collective-permute-start.55
  296.2 5.4 collective-permute-start.57
  305.6 5.4 collective-permute-start.59
  315.1 5.4 collective-permute-start.61
  324.5 5.4 collective-permute-start.63
  333.8 5.4 collective-permute-start.65
  371.4 5.4 collective-permute-start.73
  380.8 5.4 collective-permute-start.75
  390.2 5.4 collective-permute-start.77
  399.7 5.4 collective-permute-start.79
  418.6 5.4 collective-permute-start.83
  428.1 5.6 collective-permute-start.85
  449.5 521.8 %while.18 = (s32[]{:T(128)}, f32[16,512]{1,0:T(8,128)S(1)}, f32[1,16,512]{2,1,0:T(8,128)S(1)}, s32[]{:T(128)}, f32[1]{0:T(128)}, /*index=5*/f32[26,512]{1,0:T(8,...) while((s32[]{:T(128)}, f32[16,512]{1,0:T(8,128)S(1)}, ...), condition=%wide.region_25.26_spmd, body=%wide.region_22.25_spmd.sunk | while | flops 859140 | bytes 5416247 | solution.py:185
  451.5 5.4 collective-permute-done
  456.9 5.4 collective-permute-start.1
  471.2 5.4 collective-permute-done
  487.3 5.4 collective-permute-done
  503.5 5.4 collective-permute-done
  519.6 5.4 collective-permute-done
  535.8 5.4 collective-permute-done
  552.0 5.4 collective-permute-done
  568.1 5.4 collective-permute-done
  584.3 5.4 collective-permute-done
  601.5 5.4 collective-permute-done
  617.7 5.4 collective-permute-done
  633.9 5.4 collective-permute-done
  650.0 5.4 collective-permute-done
  666.2 5.4 collective-permute-done
  682.4 5.4 collective-permute-done
  698.5 5.4 collective-permute-done
  714.7 5.4 collective-permute-done
  730.8 5.4 collective-permute-done
  747.0 5.4 collective-permute-done
  763.2 5.4 collective-permute-done
  779.3 5.4 collective-permute-done
  795.5 5.4 collective-permute-done
  811.7 5.4 collective-permute-done
  827.8 5.4 collective-permute-done
  844.0 5.4 collective-permute-done
  860.2 5.4 collective-permute-done
  876.3 5.4 collective-permute-done
  892.5 5.4 collective-permute-done
  908.6 5.4 collective-permute-done
  924.8 5.4 collective-permute-done
  941.0 5.4 collective-permute-done
  957.1 5.4 collective-permute-done
  (591 shorter events, 602.3 us)
Async XLA Ops:
  0.9 54.9 %collective-permute-start.3 = (f32[1,1024]{1,0:T(1,128)S(1)}, f32[1,1024]{1,0:T(1,128)S(1)}, u32[]{:S(2)}, u32[]{:S(2)}) collective-permute-start(f32[1,1024]{1,0:T(1,128)S(1)} %bitcast.402), channel_id=1, source_target_pairs={{0,1},{1,2},{2,3},{3,4},{4,5},{5,6},{6,7},{8,9},{9,10},{10,11},{11... | collective-permute-start | bytes 12296 | tf_op jit(solution)/shard_map/ppermute | solution.py:19
  3.9 51.9 %collective-permute-start.5 = (f32[1,1024]{1,0:T(1,128)S(1)}, f32[1,1024]{1,0:T(1,128)S(1)}, u32[]{:S(2)}, u32[]{:S(2)}) collective-permute-start(f32[1,1024]{1,0:T(1,128)S(1)} %bitcast.403), channel_id=1, source_target_pairs={{1,0},{2,1},{3,2},{4,3},{5,4},{6,5},{7,6},{9,8},{10,9},{11,10},{12... | collective-permute-start | bytes 12296 | tf_op jit(solution)/shard_map/ppermute | solution.py:20
  8.8 47.0 %collective-permute-start.4 = (f32[1,1,1024]{2,1,0:T(1,128)S(1)}, f32[1,1,1024]{2,1,0:T(1,128)S(1)}, u32[]{:S(2)}, u32[]{:S(2)}) collective-permute-start(f32[1,1,1024]{2,1,0:T(1,128)S(1)} %get-tuple-element.464), channel_id=1, source_target_pairs={{0,1},{1,2},{2,3},{3,4},{4,5},{5,6},{6,7},{8,9},{9,10},{10,11},{11... | collective-permute-start | bytes 12296 | tf_op jit(solution)/shard_map/ppermute | solution.py:19
  10.8 45.1 %collective-permute-start.6 = (f32[1,1,1024]{2,1,0:T(1,128)S(1)}, f32[1,1,1024]{2,1,0:T(1,128)S(1)}, u32[]{:S(2)}, u32[]{:S(2)}) collective-permute-start(f32[1,1,1024]{2,1,0:T(1,128)S(1)} %get-tuple-element.465), channel_id=1, source_target_pairs={{1,0},{2,1},{3,2},{4,3},{5,4},{6,5},{7,6},{9,8},{10,9},{11,10},{12... | collective-permute-start | bytes 12296 | tf_op jit(solution)/shard_map/ppermute | solution.py:20
  66.1 7.4 collective-permute-start.10
  88.0 7.4 collective-permute-start.13
  97.5 7.4 collective-permute-start.15
  106.8 7.4 collective-permute-start.17
  116.3 7.6 collective-permute-start.19
  125.7 7.4 collective-permute-start.21
  135.1 7.4 collective-permute-start.23
  144.5 7.4 collective-permute-start.25
  153.9 7.4 collective-permute-start.27
  163.2 7.4 collective-permute-start.29
  172.7 7.4 collective-permute-start.31
  182.1 7.4 collective-permute-start.33
  191.5 7.4 collective-permute-start.35
  200.9 7.4 collective-permute-start.37
  210.4 7.4 collective-permute-start.39
  219.9 7.4 collective-permute-start.41
  229.3 7.4 collective-permute-start.43
  238.7 8.5 collective-permute-start.45
  247.2 7.4 collective-permute-start.46
  256.7 7.4 collective-permute-start.48
  266.1 7.4 collective-permute-start.50
  275.5 7.4 collective-permute-start.52
  284.9 7.4 collective-permute-start.54
  294.3 7.4 collective-permute-start.56
  303.7 7.4 collective-permute-start.58
  313.1 7.4 collective-permute-start.60
  322.5 7.4 collective-permute-start.62
  331.9 7.4 collective-permute-start.64
  341.3 7.4 collective-permute-start.66
  350.7 7.4 collective-permute-start.68
  360.0 7.4 collective-permute-start.70
  369.5 7.4 collective-permute-start.72
  378.9 7.4 collective-permute-start.74
  388.3 7.4 collective-permute-start.76
  397.7 7.4 collective-permute-start.78
  407.2 7.4 collective-permute-start.80
  416.7 7.4 collective-permute-start.82
  426.1 7.7 collective-permute-start.84
  440.1 8.0 collective-permute-start.86
  449.5 7.3 collective-permute-start
  456.9 7.4 collective-permute-start.1
  469.2 7.3 collective-permute-start
  485.4 7.3 collective-permute-start
  501.6 7.3 collective-permute-start
  517.7 7.3 collective-permute-start
  550.0 7.3 collective-permute-start
  566.2 7.3 collective-permute-start
  582.4 7.3 collective-permute-start
  599.6 7.3 collective-permute-start
  615.8 7.3 collective-permute-start
  631.9 7.3 collective-permute-start
  648.1 7.3 collective-permute-start
  680.4 7.3 collective-permute-start
  696.6 7.3 collective-permute-start
  712.8 7.3 collective-permute-start
  728.9 7.3 collective-permute-start
  745.1 7.3 collective-permute-start
  761.2 7.3 collective-permute-start
  777.4 7.3 collective-permute-start
  793.6 7.3 collective-permute-start
  (123 other events, 796.5 us)
where the time goes:
time: 979 us; the launch traced here: 973 us
  starting transfers between devices  558 us (57%)
  waiting for transfers between devices  325 us (33%)
  other arithmetic  35.1 us (4%)
  between operations  27.1 us (3%)
  local copies, waits for them, and re-layouts  23.9 us (2%)
    ppermute x74, starting transfers between devices, with_halo(): after = lax.ppermute(first, axis, down)  290 us
    ppermute x74, starting transfers between devices, with_halo(): before = lax.ppermute(last, axis, up)  205 us
    ppermute x33, waiting for transfers between devices, passed_along(): lax.ppermute(value, axis, [(source, source + steps) for source in range(f...  180 us
    ppermute x74, waiting for transfers between devices, with_halo(): before = lax.ppermute(last, axis, up)  99.5 us
    ppermute x33, starting transfers between devices, passed_along(): lax.ppermute(value, axis, [(source, source + steps) for source in range(f...  63.5 us
    ppermute x74, waiting for transfers between devices, with_halo(): after = lax.ppermute(first, axis, down)  46.3 us
    select_n x39, other arithmetic, sweep(): jnp.where((fine_step < counts)[:, None, None], updated, state_now)  29.5 us
  transfers between devices with their start and end apart: 181, of which 105 were waited for; matrix products, arithmetic and copies ran while one was open for 2% of the time, Pallas kernels for 0%

commit v1 on v0

v1 whole, which is shorter than its diff:
```python
import functools

import jax
import jax.numpy as jnp
from jax import lax
from jax.experimental import pallas as pl
from jax.experimental.pallas import tpu as pltpu
from jax.sharding import PartitionSpec as P

MESH = pl.DeviceIdType.MESH
STEP_MOST = 20
CSUB = 5
HALO = STEP_MOST
PAD = 24
EXT = 32 + 2 * PAD
OFF = PAD + 1
BLOCKS = EXT // 8
GROUP = 6
REACH = 2
PLAN = ((0, 3, 0, 10), (3, 11, 1, 9), (11, 19, 2, 8), (19, 20, 3, 7))


def kernel(
    dims,
    point_ref,
    init_ref,
    rate_ref,
    src_ref,
    wave_ref,
    table_ref,
    class_ref,
    steps_ref,
    out_ref,
    hist_a,
    hist_b,
    rows_rate,
    rows_src,
    weight_d,
    weight_e,
    edge,
    cond_fine,
    cond_tile,
    cond_map,
    stage,
    first,
    merge,
    split_w,
    join_w,
    own_res,
    coarse_rate,
    res_in,
    err_in,
    weight_cd,
    weight_ce,
    side_c,
    err_out,
    err_own,
    nat_rel,
    nat_err,
    s_send,
    s_halo,
    s_cond,
    s_crate,
    s_relax,
    s_res,
    s_hop,
    s_err,
):
    n_tm, n_sp, q, hs = dims
    groups = (n_tm - 2) // q
    span = 2 * hs + 1
    cext = 16 * span
    stride = cext // 8
    f32 = jnp.float32
    j = lax.axis_index("tm")
    s = lax.axis_index("space")
    pending = []

    def root_of(g):
        return (q * (g + 1) + 2) % n_tm

    def inside(t):
        return jnp.logical_and(t >= 0, t < n_sp)

    def at(cond, body):
        pl.when(cond)(body)

    group = jnp.where(j == 0, 0, (j - 1 + q) // q - 1)
    place = j - 1 - q * group
    member = jnp.logical_and(j >= 1, j <= q * groups)
    sender = j <= q * groups
    root = root_of(group)
    out_group = (j - 2 + q) // q - 1
    is_root = jnp.bool_(False)
    lead = jnp.int32(0)
    for g in range(groups):
        hit = j == root_of(g)
        is_root = jnp.logical_or(is_root, hit)
        lead = lead + jnp.where(hit, g, 0)
    reach = [d for d in range(-hs, hs + 1)]
    beside = [d for d in reach if d != 0]
    near = [-1, 0, 1]

    barrier = pltpu.get_barrier_semaphore()

    def tell(cond, tm, sp):
        def body():
            pl.semaphore_signal(barrier, inc=1, device_id=(tm, sp), device_id_type=MESH)

        at(cond, body)

    expect = jnp.int32(0)
    for d in beside:
        tell(inside(s + d), j, s + d)
        expect = expect + inside(s + d).astype(jnp.int32)
    for d in near:
        tell(jnp.logical_and(j > 0, inside(s + d)), j - 1, s + d)
        expect = expect + jnp.logical_and(j < n_tm - 1, inside(s + d)).astype(jnp.int32)
    tell(j >= 2, root_of(out_group), s)

    def greet_group():
        for d in reach:

            def body(d=d):
                for p in range(q):
                    pl.semaphore_signal(
                        barrier, inc=1, device_id=(q * lead + 1 + p, s + d), device_id_type=MESH
                    )
                pl.semaphore_signal(
                    barrier,
                    inc=1,
                    device_id=(jnp.where(lead == 0, 0, root_of(lead - 1)), s + d),
                    device_id_type=MESH,
                )

            at(inside(s + d), body)

    at(is_root, greet_group)
    strips = jnp.int32(0)
    for d in reach:
        strips = strips + inside(s + d).astype(jnp.int32)
    expect = expect + jnp.where(sender, strips, 0)
    expect = expect + jnp.where(is_root, q, 0)
    expect = expect + jnp.where(jnp.logical_and(is_root, lead < groups - 1), strips, 0)

    count = [0]

    def push(cond, src, dst, sem, tm, sp):
        slot = count[0]
        count[0] += 1

        def make():
            return pltpu.make_async_remote_copy(
                src_ref=src,
                dst_ref=dst,
                send_sem=s_send.at[slot],
                recv_sem=sem,
                device_id=(tm, sp),
                device_id_type=MESH,
            )

        at(cond, lambda: make().start())
        pending.append((cond, make))

    def arrive(cond, dst, sem):
        def body():
            pltpu.make_async_remote_copy(
                src_ref=dst,
                dst_ref=dst,
                send_sem=s_send.at[0],
                recv_sem=sem,
                device_id=(j, s),
                device_id_type=MESH,
            ).wait_recv()

        at(cond, body)

    sub = lax.broadcasted_iota(jnp.int32, (8, 128), 0)
    lane = lax.broadcasted_iota(jnp.int32, (8, 128), 1)

    def to_rows(natural, put):
        for b in range(4):
            for c in range(8):
                stage[pl.ds((b * 8 + c) * 8, 8), :] = natural[
                    pl.ds(8 * b, 8), pl.ds(128 * c, 128)
                ]
        for b in range(4):
            for i in range(8):
                put(8 * b + i, stage[pl.ds(b * 64 + i, 8, stride=8), :])

    top, bottom = s == 0, s == n_sp - 1
    up, down = s > 0, s < n_sp - 1
    zeros = jnp.zeros((PAD, 8, 128), f32)

    def put_point(r, value):
        hist_a[0, OFF + r] = value

    to_rows(point_ref.at[0], put_point)

    for i in range(4):
        fine = jnp.zeros((8, 128), f32)
        for c in range(8):
            fine = jnp.where(sub == c, table_ref[class_ref[i, c]], fine)
        cond_fine[pl.ds(32 + 8 * i, 8), :] = fine
    tile = jnp.zeros((8, 128), f32)
    for i in range(4):
        for c in range(8):
            tile = jnp.where(
                jnp.logical_and(sub == i, lane // 16 == c), table_ref[class_ref[i, c]], tile
            )
    cond_tile[hs] = tile

    def clear_top():
        hist_a[0, pl.ds(1, PAD)] = zeros
        hist_b[0, pl.ds(1, PAD)] = zeros
        rows_rate[pl.ds(0, PAD)] = zeros
        rows_src[pl.ds(0, PAD)] = zeros
        cond_fine[pl.ds(0, 32), :] = jnp.zeros((32, 128), f32)

    def clear_bottom():
        hist_a[0, pl.ds(OFF + 32, PAD)] = zeros
        hist_b[0, pl.ds(OFF + 32, PAD)] = zeros
        rows_rate[pl.ds(PAD + 32, PAD)] = zeros
        rows_src[pl.ds(PAD + 32, PAD)] = zeros
        cond_fine[pl.ds(64, 32), :] = jnp.zeros((32, 128), f32)

    at(top, clear_top)
    at(bottom, clear_bottom)

    pl.semaphore_wait(barrier, expect)

    def halos(buf, own, to_up, sems, only=None):
        a = up if only is None else jnp.logical_and(up, only)
        b = down if only is None else jnp.logical_and(down, only)
        push(a, buf.at[pl.ds(own, HALO)], buf.at[pl.ds(own + 32, HALO)], sems.at[1], j, s - 1)
        push(
            b,
            buf.at[pl.ds(own + 32 - HALO, HALO)],
            buf.at[pl.ds(own - HALO, HALO)],
            sems.at[0],
            j,
            s + 1,
        )

    def halos_in(buf, own, sems):
        arrive(up, buf.at[pl.ds(own - HALO, HALO)], sems.at[0])
        arrive(down, buf.at[pl.ds(own + 32, HALO)], sems.at[1])

    mine = cond_fine.at[pl.ds(32, 32), :]
    push(up, mine, cond_fine.at[pl.ds(64, 32), :], s_cond.at[0], j, s - 1)
    push(down, mine, cond_fine.at[pl.ds(0, 32), :], s_cond.at[1], j, s + 1)
    for d in beside:
        push(
            jnp.logical_and(is_root, inside(s + d)),
            cond_tile.at[hs],
            cond_tile.at[hs - d],
            s_crate.at[1, hs - d],
            j,
            s + d,
        )
    halos(hist_a.at[0], OFF, None, s_halo.at[0])

    def put_rate(r, value):
        rows_rate[PAD + r] = value

    def put_src(r, value):
        rows_src[PAD + r] = value

    to_rows(rate_ref, put_rate)
    halos(rows_rate, PAD, None, s_halo.at[1])
    to_rows(src_ref, put_src)
    halos(rows_src, PAD, None, s_halo.at[2])

    def place_initial():
        def put_init(r, value):
            hist_b[0, OFF + r] = value

        to_rows(init_ref, put_init)

    at(j == 0, place_initial)
    push(
        jnp.logical_and(j == 0, up),
        hist_b.at[0, pl.ds(OFF, HALO)],
        hist_b.at[0, pl.ds(OFF + 32, HALO)],
        s_relax.at[2],
        j,
        s - 1,
    )
    push(
        jnp.logical_and(j == 0, down),
        hist_b.at[0, pl.ds(OFF + 32 - HALO, HALO)],
        hist_b.at[0, pl.ds(OFF - HALO, HALO)],
        s_relax.at[0],
        j,
        s + 1,
    )

    def fill_split(i, carry):
        f = lax.broadcasted_iota(jnp.int32, (64, 512), 0) + 64 * i
        o = lax.broadcasted_iota(jnp.int32, (64, 512), 1)
        hit = jnp.logical_and((f >> 3) == (o & 127), ((f & 7) >> 1) == (o >> 7))
        split_w[pl.ds(pl.multiple_of(64 * i, 64), 64), :] = jnp.where(hit, 1.0, 0.0).astype(
            jnp.bfloat16
        )
        return carry

    def fill_join(i, carry):
        o = lax.broadcasted_iota(jnp.int32, (32, 1024), 0) + 32 * i
        f = lax.broadcasted_iota(jnp.int32, (32, 1024), 1)
        hit = jnp.logical_and((f >> 3) == (o & 127), ((f & 7) >> 1) == (o >> 7))
        join_w[pl.ds(pl.multiple_of(32 * i, 32), 32), :] = jnp.where(hit, 1.0, 0.0).astype(
            jnp.bfloat16
        )
        return carry

    lax.fori_loop(0, 16, fill_split, 0)
    lax.fori_loop(0, 16, fill_join, 0)

    def exact_dot(values, matrix):
        high = values.astype(jnp.bfloat16)
        rest = values - high.astype(f32)
        mid = rest.astype(jnp.bfloat16)
        low = (rest - mid.astype(f32)).astype(jnp.bfloat16)
        n = values.shape[0]
        parts = jnp.dot(
            jnp.concatenate([high, mid, low], axis=0), matrix, preferred_element_type=f32
        )
        return (parts[2 * n :] + parts[n : 2 * n]) + parts[:n]

    def restrict(row_pair):
        for i in range(16):
            stage[pl.ds(8 * i, 8), :] = row_pair(i)
        for b in range(2):
            for c in range(8):
                merge[pl.ds(8 * b, 8), pl.ds(128 * c, 128)] = stage[
                    pl.ds(64 * b + c, 8, stride=8), :
                ]
        return 0.25 * exact_dot(merge[...], split_w[...])

    def make_coarse_rate():
        values = restrict(lambda i: rows_rate[PAD + 2 * i] + rows_rate[PAD + 2 * i + 1])
        for m in range(4):
            coarse_rate[m, pl.ds(16 * hs, 16), :] = values[:, 128 * m : 128 * m + 128]
        for d in beside:

            def wipe(d=d):
                where = pl.ds(16 * (hs + d), 16)
                coarse_rate[:, where, :] = jnp.zeros((4, 16, 128), f32)
                err_in[:, where, :] = jnp.zeros((4, 16, 128), f32)
                for p in range(q):
                    res_in[p, :, where, :] = jnp.zeros((4, 16, 128), f32)
                cond_tile[hs + d] = jnp.zeros((8, 128), f32)

            at(jnp.logical_not(inside(s + d)), wipe)

    at(is_root, make_coarse_rate)
    for d in beside:
        push(
            jnp.logical_and(is_root, inside(s + d)),
            coarse_rate.at[:, pl.ds(16 * hs, 16), :],
            coarse_rate.at[:, pl.ds(16 * (hs - d), 16), :],
            s_crate.at[0, hs - d],
            j,
            s + d,
        )

    def add_up(i, total):
        return total + jnp.where(i < j, steps_ref[i], 0)

    start = lax.fori_loop(0, n_tm, add_up, jnp.int32(0))
    steps = steps_ref[j]

    arrive(down, cond_fine.at[pl.ds(64, 32), :], s_cond.at[0])
    arrive(up, cond_fine.at[pl.ds(0, 32), :], s_cond.at[1])
    halos_in(rows_rate, PAD, s_halo.at[1])

    for b in range(BLOCKS):
        here = cond_fine[pl.ds(8 * (b + 1), 8), :]
        safe = jnp.where(here > 0.0, here, 1.0)
        above = jnp.sqrt(cond_fine[pl.ds(8 * b, 8), :] * here) / safe
        below = jnp.sqrt(cond_fine[pl.ds(8 * (b + 2), 8), :] * here) / safe
        left = jnp.where(sub == 0, 0.0, jnp.sqrt(pltpu.roll(here, 1, 0) * here) / safe)
        right = jnp.where(sub == 7, 0.0, jnp.sqrt(pltpu.roll(here, 7, 0) * here) / safe)
        edge[b, 0] = above
        edge[b, 1] = below
        edge[b, 2] = left
        edge[b, 3] = right
        sides = jnp.where(lane == 0, left, 1.0) + jnp.where(lane == 127, right, 1.0)
        for i in range(8):
            total = sides + (above if i == 0 else 1.0) + (below if i == 7 else 1.0)
            scaled = rows_rate[8 * b + i] * here
            weight_d[8 * b + i] = scaled
            weight_e[8 * b + i] = 1.0 - scaled * total

    first_lane = lax.broadcasted_iota(jnp.int32, (8, 8, 128), 2) == 0
    last_lane = lax.broadcasted_iota(jnp.int32, (8, 8, 128), 2) == 127

    def sweep(hist):
        for n0, n1, b0, b1 in PLAN:

            def one_step(n, carry, b0=b0, b1=b1):
                amp = wave_ref[jnp.minimum(start + n, wave_ref.shape[0] - 1)]
                for b in range(b0, b1):
                    here = hist[n, pl.ds(8 * b + 1, 8)]
                    above = hist[n, pl.ds(8 * b, 8)]
                    below = hist[n, pl.ds(8 * b + 2, 8)]
                    above = jnp.concatenate([above[:1] * edge[b, 0][None], above[1:]], axis=0)
                    below = jnp.concatenate([below[:7], below[7:] * edge[b, 1][None]], axis=0)
                    left = pltpu.roll(here, 1, 2)
                    right = pltpu.roll(here, 127, 2)
                    left = jnp.where(first_lane, pltpu.roll(left, 1, 1) * edge[b, 2][None], left)
                    right = jnp.where(last_lane, pltpu.roll(right, 7, 1) * edge[b, 3][None], right)
                    hist[n + 1, pl.ds(8 * b + 1, 8)] = (
                        weight_e[pl.ds(8 * b, 8)] * here
                        + weight_d[pl.ds(8 * b, 8)] * ((above + below) + (left + right))
                        + amp * rows_src[pl.ds(8 * b, 8)]
                    )
                return carry

            lax.fori_loop(n0, n1, one_step, 0)

    halos_in(hist_a.at[0], OFF, s_halo.at[0])
    halos_in(rows_src, PAD, s_halo.at[2])
    sweep(hist_a)
    for i in range(32):
        first[i] = hist_a[steps, OFF + i]

    follow = j < n_tm - 1
    push(
        jnp.logical_and(follow, up),
        first.at[pl.ds(0, HALO)],
        hist_b.at[0, pl.ds(OFF + 32, HALO)],
        s_relax.at[2],
        j + 1,
        s - 1,
    )
    push(
        jnp.logical_and(follow, down),
        first.at[pl.ds(32 - HALO, HALO)],
        hist_b.at[0, pl.ds(OFF - HALO, HALO)],
        s_relax.at[0],
        j + 1,
        s + 1,
    )
    push(follow, first, hist_b.at[0, pl.ds(OFF, 32)], s_relax.at[1], j + 1, s)
    arrive(j > 0, hist_b.at[0, pl.ds(OFF, 32)], s_relax.at[1])
    arrive(up, hist_b.at[0, pl.ds(OFF - HALO, HALO)], s_relax.at[0])
    arrive(down, hist_b.at[0, pl.ds(OFF + 32, HALO)], s_relax.at[2])
    sweep(hist_b)

    def difference(i):
        return (hist_b[steps, OFF + 2 * i] - first[2 * i]) + (
            hist_b[steps, OFF + 2 * i + 1] - first[2 * i + 1]
        )

    change = restrict(difference)
    for m in range(4):
        own_res[m] = change[:, 128 * m : 128 * m + 128]
    wide = (q - 1 - place) * CSUB
    for d in reach:
        t_in = inside(s + d)
        for rows, low, high in ((16, 8, 1 << 20), (8, 0, 8)):
            if d == 0:
                if rows == 8:
                    continue
                cond = jnp.bool_(True)
            else:
                least = 16 * (abs(d) - 1)
                cond = jnp.logical_and(wide > least + low, wide <= least + high)
            begin = 16 - rows if d > 0 else 0
            push(
                jnp.logical_and(jnp.logical_and(member, t_in), cond),
                own_res.at[:, pl.ds(begin, rows), :],
                res_in.at[jnp.clip(place, 0, q - 1), :, pl.ds(16 * (hs - d) + begin, rows), :],
                s_res.at[jnp.clip(place, 0, q - 1), hs - d],
                root,
                s + d,
            )
        push(
            jnp.logical_and(j == 0, t_in),
            own_res,
            err_in.at[:, pl.ds(16 * (hs - d), 16), :],
            s_hop.at[hs - d],
            root,
            s + d,
        )
    push(j == 0, own_res, err_own, s_err, j + 1, s)

    leads = jnp.logical_and(is_root, jnp.bool_(True))

    def lead_setup():
        for d in reach:
            for h in range(2):
                cond_map[pl.ds(8 + 16 * (hs + d) + 8 * h, 8), :] = jnp.where(
                    sub < 4,
                    cond_tile[hs + d, pl.ds(2 * h, 1), :],
                    cond_tile[hs + d, pl.ds(2 * h + 1, 1), :],
                )
        cond_map[pl.ds(0, 8), :] = jnp.zeros((8, 128), f32)
        cond_map[pl.ds(8 + cext, 8), :] = jnp.zeros((8, 128), f32)
        factors = [steps_ref[q * lead + 1 + p].astype(f32) / (4.0 * CSUB) for p in range(q)]
        for k in range(stride):
            here = cond_map[pl.ds(8 + k, 8, stride=stride), :]
            safe = jnp.where(here > 0.0, here, 1.0)
            above = jnp.sqrt(cond_map[pl.ds(7 + k, 8, stride=stride), :] * here) / safe
            below = jnp.sqrt(cond_map[pl.ds(9 + k, 8, stride=stride), :] * here) / safe
            left = jnp.where(lane == 0, 0.0, jnp.sqrt(pltpu.roll(here, 1, 1) * here) / safe)
            right = jnp.where(lane == 127, 0.0, jnp.sqrt(pltpu.roll(here, 127, 1) * here) / safe)
            side_c[0, k] = above
            side_c[1, k] = below
            side_c[2, k] = left
            side_c[3, k] = right
            for m in range(4):
                total = (above + below) + (
                    (left if m == 0 else 1.0) + (right if m == 3 else 1.0)
                )
                scaled = coarse_rate[m, pl.ds(k, 8, stride=stride), :] * here
                for p in range(q):
                    weight_cd[p, 4 * k + m] = scaled * factors[p]
                    weight_ce[p, 4 * k + m] = 1.0 - scaled * factors[p] * total

    for d in beside:
        arrive(
            jnp.logical_and(leads, inside(s + d)),
            coarse_rate.at[:, pl.ds(16 * (hs + d), 16), :],
            s_crate.at[0, hs + d],
        )
        arrive(jnp.logical_and(leads, inside(s + d)), cond_tile.at[hs + d], s_crate.at[1, hs + d])
    at(leads, lead_setup)

    for d in reach:
        arrive(
            jnp.logical_and(leads, inside(s + d)),
            err_in.at[:, pl.ds(16 * (hs + d), 16), :],
            s_hop.at[hs + d],
        )

    def coarse_steps(p, source):
        def one(i, state):
            new = []
            for k in range(stride):
                for m in range(4):
                    v = state[4 * k + m]
                    if k > 0:
                        above = state[4 * (k - 1) + m]
                    else:
                        above = pltpu.roll(state[4 * (stride - 1) + m], 1, 0)
                    if k < stride - 1:
                        below = state[4 * (k + 1) + m]
                    else:
                        below = pltpu.roll(state[m], 7, 0)
                    if m > 0:
                        left = state[4 * k + m - 1]
                    else:
                        left = pltpu.roll(state[4 * k + 3], 1, 1) * side_c[2, k]
                    if m < 3:
                        right = state[4 * k + m + 1]
                    else:
                        right = pltpu.roll(state[4 * k], 127, 1) * side_c[3, k]
                    around = (above * side_c[0, k] + below * side_c[1, k]) + (left + right)
                    new.append(weight_ce[p, 4 * k + m] * v + weight_cd[p, 4 * k + m] * around)
            return tuple(new)

        state = tuple(
            source[m, pl.ds(k, 8, stride=stride), :]
            for k in range(stride)
            for m in range(4)
        )
        state = lax.fori_loop(0, CSUB, one, state)
        for k in range(stride):
            for m in range(4):
                where = (p, m, pl.ds(k, 8, stride=stride), slice(None))
                err_out[where] = state[4 * k + m] + res_in[where]

    for p in range(q):
        wide_p = (q - 1 - p) * CSUB
        for d in reach:
            if d != 0 and wide_p <= 16 * (abs(d) - 1):
                continue
            rows = 16 if d == 0 or wide_p > 16 * (abs(d) - 1) + 8 else 8
            begin = 16 - rows if d < 0 else 0
            arrive(
                jnp.logical_and(leads, inside(s + d)),
                res_in.at[p, :, pl.ds(16 * (hs + d) + begin, rows), :],
                s_res.at[p, hs + d],
            )
        source = err_in if p == 0 else err_out.at[p - 1]
        at(leads, functools.partial(coarse_steps, p, source))
        own = err_out.at[p, :, pl.ds(16 * hs, 16), :]
        if p == q - 1:
            for d in reach:
                push(
                    jnp.logical_and(jnp.logical_and(leads, lead < groups - 1), inside(s + d)),
                    own,
                    err_in.at[:, pl.ds(16 * (hs - d), 16), :],
                    s_hop.at[hs - d],
                    root_of(lead + 1),
                    s + d,
                )
        push(leads, own, err_own, s_err, q * lead + 2 + p, s)

    for i in range(32):
        stage[pl.ds(8 * i, 8), :] = hist_b[0, OFF + i]
    for b in range(4):
        for c in range(8):
            nat_rel[pl.ds(8 * b, 8), pl.ds(128 * c, 128)] = stage[
                pl.ds(64 * b + c, 8, stride=8), :
            ]

    def no_error():
        out_ref[0] = nat_rel[...]

    def with_error():
        errors = jnp.concatenate([err_own[m] for m in range(4)], axis=1)
        spread = exact_dot(errors, join_w[...])
        for c in range(8):
            columns = slice(128 * c, 128 * c + 128)
            nat_err[c, pl.ds(0, 16, stride=2), :] = spread[:, columns]
            nat_err[c, pl.ds(1, 16, stride=2), :] = spread[:, columns]
            out_ref[0, :, pl.ds(128 * c, 128)] = nat_rel[:, pl.ds(128 * c, 128)] + nat_err[c]

    arrive(j > 0, err_own, s_err)
    at(j == 0, no_error)
    at(j > 0, with_error)
    for cond, make in pending:
        at(cond, lambda make=make: make().wait_send())


def advance(dims, *args):
    n_tm, n_sp, q, hs = dims
    span = 2 * hs + 1
    cext = 16 * span
    planes = cext // 2
    f32 = jnp.float32
    vm = pl.BlockSpec(memory_space=pltpu.VMEM)
    sm = pl.BlockSpec(memory_space=pltpu.SMEM)
    dma = pltpu.SemaphoreType.DMA
    return pl.pallas_call(
        functools.partial(kernel, dims),
        out_shape=jax.ShapeDtypeStruct((1, 32, 1024), f32),
        in_specs=[vm] * 4 + [sm] * 4,
        out_specs=vm,
        scratch_shapes=[
            pltpu.VMEM((STEP_MOST + 1, EXT + 2, 8, 128), f32),
            pltpu.VMEM((STEP_MOST + 1, EXT + 2, 8, 128), f32),
            pltpu.VMEM((EXT, 8, 128), f32),
            pltpu.VMEM((EXT, 8, 128), f32),
            pltpu.VMEM((EXT, 8, 128), f32),
            pltpu.VMEM((EXT, 8, 128), f32),
            pltpu.VMEM((BLOCKS, 4, 8, 128), f32),
            pltpu.VMEM((96, 128), f32),
            pltpu.VMEM((span, 8, 128), f32),
            pltpu.VMEM((cext + 16, 128), f32),
            pltpu.VMEM((256, 128), f32),
            pltpu.VMEM((32, 8, 128), f32),
            pltpu.VMEM((16, 1024), f32),
            pltpu.VMEM((1024, 512), jnp.bfloat16),
            pltpu.VMEM((512, 1024), jnp.bfloat16),
            pltpu.VMEM((4, 16, 128), f32),
            pltpu.VMEM((4, cext, 128), f32),
            pltpu.VMEM((q, 4, cext, 128), f32),
            pltpu.VMEM((4, cext, 128), f32),
            pltpu.VMEM((q, planes, 8, 128), f32),
            pltpu.VMEM((q, planes, 8, 128), f32),
            pltpu.VMEM((4, cext // 8, 8, 128), f32),
            pltpu.VMEM((q, 4, cext, 128), f32),
            pltpu.VMEM((4, 16, 128), f32),
            pltpu.VMEM((32, 1024), f32),
            pltpu.VMEM((8, 32, 128), f32),
            dma((80,)),
            dma((3, 2)),
            dma((2,)),
            dma((2, span)),
            dma((3,)),
            dma((q, span)),
            dma((span,)),
            dma(()),
        ],
        compiler_params=pltpu.CompilerParams(
            collective_id=0, has_side_effects=True, vmem_limit_bytes=48 * 1024 * 1024
        ),
    )(*args)


def solution(mesh, q=GROUP, hs=REACH):
    placed = (
        P("tm", "space", None),
        P("space", None),
        P("space", None),
        P("space", None),
        P(),
        P(),
        P("space", None),
        P(),
    )
    dims = (mesh.shape["tm"], mesh.shape["space"], q, hs)
    return jax.shard_map(
        functools.partial(advance, dims),
        mesh=mesh,
        in_specs=placed,
        out_specs=P("tm", "space", None),
        check_vma=False,
    )
```

time: 979 us -> 83.2 us (0.08)
  the two profiles are of different devices: /device:TPU:136 before, /device:TPU:31 now
where the time goes in v1:
time: 83.2 us; the launch traced here: 83 us
  Pallas kernels  76 us (91%)
  local copies, waits for them, and re-layouts  6.94 us (8%)
    pallas_call x1, Pallas kernels, advance(): pl.pallas_call(functools.partial(kernel, dims), out_shape=jax.ShapeDtypeS...  76 us
    unnamed x17, local copies, waits for them, and re-layouts  6.94 us

profile of v1, /device:TPU:31, one launch (start us, length us, event | category | flops | bytes accessed | tf_op | source)
XLA Modules:
  0.0 83.0 jit_solution(8194936756357030841)
XLA Ops:
  0.0 0.0 copy-start
  0.0 0.9 %copy-done = f32[1,32,1024]{2,1,0:T(8,128)S(1)} copy-done((f32[1,32,1024]{2,1,0:T(8,128)S(1)}, f32[1,32,1024]{2,1,0:T(8,128)}, u32[]{:S(2)}) %copy-start) | copy-done | bytes 131096
  0.9 0.0 copy-start.1
  0.9 0.9 %copy-done.1 = f32[32,1024]{1,0:T(8,128)S(1)} copy-done((f32[32,1024]{1,0:T(8,128)S(1)}, f32[32,1024]{1,0:T(8,128)}, u32[]{:S(2)}) %copy-start.1) | copy-done | bytes 131096
  1.8 0.0 copy-start.2
  1.8 0.9 %copy-done.2 = f32[32,1024]{1,0:T(8,128)S(1)} copy-done((f32[32,1024]{1,0:T(8,128)S(1)}, f32[32,1024]{1,0:T(8,128)}, u32[]{:S(2)}) %copy-start.2) | copy-done | bytes 131096
  2.7 0.0 copy-start.3
  2.7 0.9 %copy-done.3 = f32[32,1024]{1,0:T(8,128)S(1)} copy-done((f32[32,1024]{1,0:T(8,128)S(1)}, f32[32,1024]{1,0:T(8,128)}, u32[]{:S(2)}) %copy-start.3) | copy-done | bytes 131096
  3.6 0.0 copy-start.4
  3.6 0.7 copy-done.4
  4.3 0.0 copy-start.5
  4.3 0.7 copy-done.5
  5.0 0.0 copy-start.6
  5.0 0.7 copy-done.6
  5.6 0.0 copy-start.7
  5.6 0.7 copy-done.7
  6.3 76.0 %shard_map.82 = f32[1,32,1024]{2,1,0:T(8,128)S(1)} custom-call(f32[1,32,1024]{2,1,0:T(8,128)S(1)} %copy-done, f32[32,1024]{1,0:T(8,128)S(1)} %copy-done.1, f32[32,1024]{1,0:T(8,128)S(1)} %copy-done.2, f32[32,1024]{1,0:T(8,128)S(1)} %copy-done.3, f32[512]{0:T(512)S(1)} %copy-done.4, f32[16]{0:T(128)S(1)} %copy-done.6, s32[4,8]{1,0:T(4,128)S(1)} %copy-done.5, ...), custom_call_target="tpu_custom_call" | custom-call | tf_op jit(solution)/shard_map/pallas_call | solution.py:638
  82.3 0.7 copy.10
Async XLA Ops:
  0.0 0.9 %copy-start = (f32[1,32,1024]{2,1,0:T(8,128)S(1)}, f32[1,32,1024]{2,1,0:T(8,128)}, u32[]{:S(2)}) copy-start(f32[1,32,1024]{2,1,0:T(8,128)} %point_ref.1) | copy-start | bytes 393220
  0.9 0.9 %copy-start.1 = (f32[32,1024]{1,0:T(8,128)S(1)}, f32[32,1024]{1,0:T(8,128)}, u32[]{:S(2)}) copy-start(f32[32,1024]{1,0:T(8,128)} %init_ref.1) | copy-start | bytes 393220
  1.8 0.9 %copy-start.2 = (f32[32,1024]{1,0:T(8,128)S(1)}, f32[32,1024]{1,0:T(8,128)}, u32[]{:S(2)}) copy-start(f32[32,1024]{1,0:T(8,128)} %rate_ref.1) | copy-start | bytes 393220
  2.7 0.9 %copy-start.3 = (f32[32,1024]{1,0:T(8,128)S(1)}, f32[32,1024]{1,0:T(8,128)}, u32[]{:S(2)}) copy-start(f32[32,1024]{1,0:T(8,128)} %src_ref.1) | copy-start | bytes 393220
  3.6 0.7 copy-start.4
  4.3 0.7 copy-start.5
  5.0 0.7 copy-start.6
  5.6 0.7 copy-start.7

commit v2 on v0

v2 whole, which is shorter than its diff:
```python
import functools

import jax
import jax.numpy as jnp
from jax import lax
from jax.experimental import pallas as pl
from jax.experimental.pallas import tpu as pltpu
from jax.sharding import PartitionSpec as P

MESH = pl.DeviceIdType.MESH
STEP_MOST = 20
CSUB = 5
HALO = 24
EXT = 32 + 2 * HALO
OFF = 8
BLOCKS = EXT // 8
PLAN = ((0, 2, 0, 10), (2, 6, 1, 9), (6, 10, 2, 8))
GROUPS = (4, 13, 13)
LEADS = (6, 4, 12)


def kernel(
    dims,
    point_ref,
    init_ref,
    rate_ref,
    src_ref,
    wave_hbm,
    table_hbm,
    class_hbm,
    steps_hbm,
    out_ref,
    wave_ref,
    table_ref,
    class_ref,
    steps_ref,
    nat_point,
    nat_rate,
    nat_src,
    nat_init,
    hist_a,
    hist_b,
    hist_c,
    rows_rate,
    rows_src,
    weight_d,
    weight_e,
    edge,
    tiles,
    first,
    change,
    perm_w,
    back_w,
    join_w,
    own_res,
    coarse_rate,
    res_in,
    err_in,
    weight_cd,
    weight_ce,
    side_c,
    even,
    odd,
    even_turn,
    odd_turn,
    err_out,
    err_own,
    nat_rel,
    nat_err,
    s_local,
    s_send,
    s_errs,
    s_point,
    s_static,
    s_share,
    s_tile,
    s_crate,
    s_relax,
    s_res,
    s_hop,
    s_err,
):
    n_tm, n_sp, sizes, heads = dims
    groups = len(sizes)
    starts_of = [1 + sum(sizes[:g]) for g in range(groups + 1)]
    f32 = jnp.float32
    bf16 = jnp.bfloat16
    i32 = jnp.int32
    j = lax.axis_index("tm")
    s = lax.axis_index("space")
    twin = j + 1 - 2 * (j % 2)
    pending = []

    def at(cond, body):
        pl.when(cond)(body)

    def both(a, b):
        return jnp.logical_and(a, b)

    def pick(values, index):
        out = i32(values[0])
        for g in range(1, len(values)):
            out = jnp.where(index == g, i32(values[g]), out)
        return out

    def reach_of(rows):
        return (rows + 15) // 16

    def close(t, reach):
        return both(t - s <= reach, s - t <= reach)

    group = i32(0)
    out_group = i32(0)
    for g in range(1, groups):
        group = group + (j >= starts_of[g]).astype(i32)
        out_group = out_group + (j >= starts_of[g] + 1).astype(i32)
    sender = j < starts_of[groups]
    place = j - pick(starts_of, group)
    root = pick(heads, group)
    reach_res = jnp.where(
        j == 0, reach_of(CSUB * sizes[0]), reach_of((pick(sizes, group) - 1 - place) * CSUB)
    )
    is_root = jnp.bool_(False)
    lead = i32(0)
    for g in range(groups):
        is_root = jnp.logical_or(is_root, j == heads[g])
        lead = lead + jnp.where(j == heads[g], g, 0)
    lead_size = pick(sizes, lead)
    lead_start = pick(starts_of, lead)
    has_next = both(is_root, lead < groups - 1)
    next_lead = jnp.minimum(lead + 1, groups - 1)
    next_root = pick(heads, next_lead)
    reach_next = reach_of(CSUB * pick(sizes, next_lead))
    reach_here = reach_of(CSUB * lead_size)

    top, bottom = s == 0, s == n_sp - 1
    up, down = s > 0, s < n_sp - 1

    loads = [
        pltpu.make_async_copy(class_hbm, class_ref, s_local.at[0]),
        pltpu.make_async_copy(table_hbm, table_ref, s_local.at[1]),
        pltpu.make_async_copy(rate_ref, nat_rate.at[pl.ds(HALO, 32), :], s_local.at[2]),
        pltpu.make_async_copy(src_ref, nat_src.at[pl.ds(HALO, 32), :], s_local.at[3]),
        pltpu.make_async_copy(point_ref.at[0], nat_point.at[pl.ds(HALO, 32), :], s_local.at[4]),
        pltpu.make_async_copy(init_ref, nat_init, s_local.at[5]),
        pltpu.make_async_copy(steps_hbm, steps_ref, s_local.at[6]),
        pltpu.make_async_copy(wave_hbm, wave_ref, s_local.at[7]),
    ]
    for load in loads:
        load.start()

    barrier = pltpu.get_barrier_semaphore()
    expect = i32(1)

    def signal(tm, sp):
        pl.semaphore_signal(barrier, inc=1, device_id=(tm, sp), device_id_type=MESH)

    def tell(cond, tm, sp):
        at(cond, lambda: signal(tm, sp))

    signal(twin, s)
    for t in range(n_sp):
        beside = both(t != s, jnp.logical_or(is_root, close(t, 1)))
        tell(beside, j, t)
        tell(both(j > 0, close(t, 1)), j - 1, t)
        expect = expect + beside.astype(i32)
        expect = expect + both(j < n_tm - 1, close(t, 1)).astype(i32)
        expect = expect + both(sender, close(t, reach_res)).astype(i32)
        expect = expect + both(has_next, close(t, reach_next)).astype(i32)
    tell(j >= 2, pick(heads, out_group), s)
    expect = expect + jnp.where(is_root, lead_size, 0)

    def greet_group():
        before = jnp.where(lead == 0, 0, pick(heads, jnp.maximum(lead - 1, 0)))
        for t in range(n_sp):
            tell(close(t, reach_here), before, t)

        def one(p, carry):
            reach = reach_of((lead_size - 1 - p) * CSUB)
            for t in range(n_sp):
                tell(close(t, reach), lead_start + p, t)
            return carry

        lax.fori_loop(0, lead_size, one, 0)

    at(is_root, greet_group)

    count = [0]

    def push(cond, src, dst, sem, tm, sp):
        slot = count[0]
        count[0] += 1

        def make():
            return pltpu.make_async_remote_copy(
                src_ref=src,
                dst_ref=dst,
                send_sem=s_send.at[slot],
                recv_sem=sem,
                device_id=(tm, sp),
                device_id_type=MESH,
            )

        at(cond, lambda: make().start())
        pending.append((cond, make))

    def arrive(cond, dst, sem):
        def body():
            pltpu.make_async_remote_copy(
                src_ref=dst,
                dst_ref=dst,
                send_sem=s_send.at[0],
                recv_sem=sem,
                device_id=(j, s),
                device_id_type=MESH,
            ).wait_recv()

        at(cond, body)

    sub = lax.broadcasted_iota(i32, (8, 128), 0)
    lane = lax.broadcasted_iota(i32, (8, 128), 1)
    above_rows, own_rows, below_rows = pl.ds(0, HALO), pl.ds(HALO, 32), pl.ds(HALO + 32, HALO)
    h_above, h_own, h_below = pl.ds(OFF, HALO), pl.ds(OFF + HALO, 32), pl.ds(OFF + HALO + 32, HALO)

    def clear(where, h_where, tile):
        for buf in (nat_point, nat_rate, nat_src):
            buf[where, :] = jnp.zeros((HALO, 1024), f32)
        hist_c[0, :, h_where, :] = jnp.zeros((8, HALO, 128), f32)
        tiles[pl.ds(8 * tile, 8), :] = jnp.zeros((8, 128), f32)

    at(top, lambda: clear(above_rows, h_above, 0))
    at(bottom, lambda: clear(below_rows, h_below, n_sp + 1))

    loads[0].wait()
    loads[1].wait()
    tile = jnp.zeros((8, 128), f32)
    for i in range(4):
        for c in range(8):
            tile = jnp.where(both(sub == i, lane // 16 == c), table_ref[class_ref[i, c]], tile)
    my_tile = tiles.at[pl.ds(pl.multiple_of(8 * s + 8, 8), 8), :]
    my_tile[...] = tile

    def fill_perm(i, carry):
        f = lax.broadcasted_iota(i32, (64, 1024), 0) + 64 * i
        o = lax.broadcasted_iota(i32, (64, 1024), 1)
        hit = o == ((f & 7) << 7) + (f >> 3)
        perm_w[pl.ds(pl.multiple_of(64 * i, 64), 64), :] = jnp.where(hit, 1.0, 0.0).astype(bf16)
        return carry

    lax.fori_loop(0, 16, fill_perm, 0)

    pl.semaphore_wait(barrier, expect)

    for t in range(n_sp):
        push(
            both(t != s, jnp.logical_or(is_root, close(t, 1))), my_tile, my_tile, s_tile.at[s], j, t
        )
    low, high = pl.ds(0, HALO), pl.ds(32 - HALO, HALO)
    first_core, second_core = j % 2 == 0, j % 2 == 1
    for core, ref, nat in ((first_core, rate_ref, nat_rate), (second_core, src_ref, nat_src)):
        push(both(core, up), ref.at[low, :], nat.at[below_rows, :], s_static.at[1], j, s - 1)
        push(both(core, down), ref.at[high, :], nat.at[above_rows, :], s_static.at[0], j, s + 1)
    push(up, point_ref.at[0, low, :], nat_point.at[below_rows, :], s_point.at[1], j, s - 1)
    push(down, point_ref.at[0, high, :], nat_point.at[above_rows, :], s_point.at[0], j, s + 1)

    def exact_dot(values, matrix):
        large = values.astype(bf16)
        rest = values - large.astype(f32)
        mid = rest.astype(bf16)
        small = (rest - mid.astype(f32)).astype(bf16)
        n = values.shape[0]
        parts = jnp.dot(
            jnp.concatenate([large, mid, small], axis=0), matrix[...], preferred_element_type=f32
        )
        return (parts[2 * n :] + parts[n : 2 * n]) + parts[:n]

    def to_parts(nat, put):
        moved = exact_dot(nat[own_rows, :], perm_w)
        for m in range(8):
            put(m, 0, moved[:, 128 * m : 128 * m + 128])

    def halos_to_parts(nat, put):
        moved = exact_dot(jnp.concatenate([nat[above_rows, :], nat[below_rows, :]], axis=0), perm_w)
        for m in range(8):
            columns = slice(128 * m, 128 * m + 128)
            put(m, -1, moved[:HALO, columns])
            put(m, 1, moved[HALO:, columns])

    rows_at = {-1: above_rows, 0: own_rows, 1: below_rows}
    h_rows_at = {-1: h_above, 0: h_own, 1: h_below}

    def put_in(ref):
        def put(m, which, value):
            ref[m, rows_at[which], :] = value

        return put

    def put_point(m, which, value):
        hist_a[0, m, h_rows_at[which], :] = value

    loads[2].wait()
    to_parts(nat_rate, put_in(rows_rate))

    mine16 = pl.ds(pl.multiple_of(16 * s, 16), 16)

    def make_coarse_rate():
        for m in range(4):
            parts = []
            for side in (0, 1):
                part = rows_rate.at[2 * m + side]
                a = part[pl.ds(HALO, 16, stride=2), :]
                parts.append(a + part[pl.ds(HALO + 1, 16, stride=2), :])
            coarse_rate[m, mine16, :] = 0.25 * (parts[0] + parts[1])

    at(is_root, make_coarse_rate)
    for t in range(n_sp):
        strip = coarse_rate.at[:, mine16, :]
        push(both(is_root, t != s), strip, strip, s_crate.at[s], j, t)

    loads[3].wait()
    to_parts(nat_src, put_in(rows_src))
    loads[4].wait()
    to_parts(nat_point, put_point)
    loads[5].wait()

    def place_initial():
        moved = exact_dot(nat_init[...], perm_w)
        for m in range(8):
            hist_c[0, m, h_own, :] = moved[:, 128 * m : 128 * m + 128]

    at(j == 0, place_initial)
    at_c = hist_c.at[0]
    push(
        both(j == 0, up),
        at_c.at[:, pl.ds(OFF + HALO, HALO), :],
        at_c.at[:, h_below, :],
        s_relax.at[2],
        j,
        s - 1,
    )
    push(
        both(j == 0, down),
        at_c.at[:, pl.ds(OFF + 32, HALO), :],
        at_c.at[:, h_above, :],
        s_relax.at[0],
        j,
        s + 1,
    )

    def fill_back(i, carry):
        o = lax.broadcasted_iota(i32, (64, 1024), 0) + 64 * i
        f = lax.broadcasted_iota(i32, (64, 1024), 1)
        hit = f == ((o & 127) << 3) + (o >> 7)
        back_w[pl.ds(pl.multiple_of(64 * i, 64), 64), :] = jnp.where(hit, 1.0, 0.0).astype(bf16)
        return carry

    def fill_join(i, carry):
        o = lax.broadcasted_iota(i32, (64, 1024), 0) + 64 * i
        f = lax.broadcasted_iota(i32, (64, 1024), 1)
        hit = (f >> 1) == ((o & 127) << 2) + (o >> 7)
        join_w[pl.ds(pl.multiple_of(64 * i, 64), 64), :] = jnp.where(hit, 1.0, 0.0).astype(bf16)
        return carry

    lax.fori_loop(0, 16, fill_back, 0)
    lax.fori_loop(0, 8, fill_join, 0)

    loads[6].wait()
    loads[7].wait()

    def add_up(i, total):
        return total + jnp.where(i < j, steps_ref[i], 0)

    start = lax.fori_loop(0, n_tm, add_up, i32(0))
    steps = steps_ref[j]

    for core, nat, other in ((first_core, nat_rate, nat_src), (second_core, nat_src, nat_rate)):
        for side, where, sem in ((up, above_rows, 0), (down, below_rows, 1)):
            cond = both(core, side)
            arrive(cond, nat.at[where, :], s_static.at[sem])
            push(cond, nat.at[where, :], nat.at[where, :], s_share.at[sem], twin, s)
    for t in range(n_sp):
        arrive(both(t != s, close(t, 1)), tiles.at[pl.ds(8 * t + 8, 8), :], s_tile.at[t])

    def block_row(b):
        strip, row = (b + 1) // 4, (b + 1) % 4
        line = tiles[pl.ds(pl.multiple_of(8 * s + 8 * strip, 8), 8), :][row : row + 1, :]
        return jnp.broadcast_to(line, (8, 128))

    for b in range(BLOCKS):
        here = block_row(b)
        safe = jnp.where(here > 0.0, here, 1.0)
        edge[b, 0] = jnp.where(sub == 0, jnp.sqrt(block_row(b - 1) * here) / safe, 1.0)
        edge[b, 1] = jnp.where(sub == 7, jnp.sqrt(block_row(b + 1) * here) / safe, 1.0)
        edge[b, 2] = jnp.where(lane == 0, 0.0, jnp.sqrt(pltpu.roll(here, 1, 1) * here) / safe)
        edge[b, 3] = jnp.where(lane == 127, 0.0, jnp.sqrt(pltpu.roll(here, 127, 1) * here) / safe)
        edge[b, 4] = here

    def weigh(blocks):
        for b in blocks:
            rows = pl.ds(8 * b, 8)
            here = edge[b, 4]
            ends = edge[b, 0] + edge[b, 1]
            for m in range(8):
                total = ends + (
                    (edge[b, 2] if m == 0 else 1.0) + (edge[b, 3] if m == 7 else 1.0)
                )
                scaled = rows_rate[m, rows, :] * here
                weight_d[m, rows, :] = scaled
                weight_e[m, rows, :] = 1.0 - scaled * total

    weigh(range(3, 7))
    for core, nat in ((first_core, nat_src), (second_core, nat_rate)):
        for side, where, sem in ((up, above_rows, 0), (down, below_rows, 1)):
            arrive(both(core, side), nat.at[where, :], s_share.at[sem])
    halos_to_parts(nat_rate, put_in(rows_rate))
    halos_to_parts(nat_src, put_in(rows_src))
    weigh((0, 1, 2, 7, 8, 9))
    arrive(up, nat_point.at[above_rows, :], s_point.at[0])
    arrive(down, nat_point.at[below_rows, :], s_point.at[1])
    halos_to_parts(nat_point, put_point)

    def half(read, write, amp, b0, b1):
        for b in range(b0, b1):
            r0 = OFF + 8 * b
            rows = pl.ds(8 * b, 8)
            cur = [read[m, pl.ds(r0, 8), :] for m in range(8)]
            far_left = pltpu.roll(cur[7], 1, 1) * edge[b, 2]
            far_right = pltpu.roll(cur[0], 127, 1) * edge[b, 3]
            for m in (1, 2, 3, 4, 5, 6, 0, 7):
                left = cur[m - 1] if m > 0 else far_left
                right = cur[m + 1] if m < 7 else far_right
                above = read[m, pl.ds(r0 - 1, 8), :] * edge[b, 0]
                below = read[m, pl.ds(r0 + 1, 8), :] * edge[b, 1]
                write[m, pl.ds(r0, 8), :] = (
                    weight_e[m, rows, :] * cur[m]
                    + weight_d[m, rows, :] * ((above + below) + (left + right))
                    + amp * rows_src[m, rows, :]
                )

    def sweep(hist):
        last = wave_ref.shape[0] - 1
        for k0, k1, b0, b1 in PLAN:

            def two_steps(k, carry, b0=b0, b1=b1):
                half(hist.at[k], hist_b.at[k], wave_ref[jnp.minimum(start + 2 * k, last)], b0, b1)
                half(
                    hist_b.at[k],
                    hist.at[k + 1],
                    wave_ref[jnp.minimum(start + 2 * k + 1, last)],
                    b0,
                    b1,
                )
                return carry

            lax.fori_loop(k0, k1, two_steps, 0)

    pair = steps >> 1
    odd_count = (steps & 1) == 1

    def state_after(hist, m, where):
        return jnp.where(odd_count, hist_b[pair, m, where, :], hist[pair, m, where, :])

    sweep(hist_a)
    for m in range(8):
        first[m] = state_after(hist_a, m, h_own)

    follow = j < n_tm - 1
    push(
        both(follow, up), first.at[:, low, :], at_c.at[:, h_below, :], s_relax.at[2], j + 1, s - 1
    )
    push(
        both(follow, down), first.at[:, high, :], at_c.at[:, h_above, :], s_relax.at[0], j + 1, s + 1
    )
    push(follow, first, at_c.at[:, h_own, :], s_relax.at[1], j + 1, s)
    arrive(j > 0, at_c.at[:, h_own, :], s_relax.at[1])
    arrive(up, at_c.at[:, h_above, :], s_relax.at[0])
    arrive(down, at_c.at[:, h_below, :], s_relax.at[2])
    sweep(hist_c)

    for m in range(8):
        change[m] = state_after(hist_c, m, h_own) - first[m]
    for m in range(4):
        parts = []
        for side in (0, 1):
            part = change.at[2 * m + side]
            parts.append(part[pl.ds(0, 16, stride=2), :] + part[pl.ds(1, 16, stride=2), :])
        own_res[m] = 0.25 * (parts[0] + parts[1])
    slot = jnp.clip(place, 0, max(sizes) - 1)
    for t in range(n_sp):
        cond = both(sender, close(t, reach_res))
        push(both(cond, j > 0), own_res, res_in.at[slot, :, mine16, :], s_res.at[slot, s], root, t)
        push(both(cond, j == 0), own_res, err_in.at[:, mine16, :], s_hop.at[s], root, t)
    push(j == 0, own_res, err_own, s_err, j + 1, s)

    def lead_setup():
        block = [tiles[pl.ds(8 + i, n_sp, stride=8), :] for i in range(4)]
        if n_sp < 8:
            rest = jnp.zeros((8 - n_sp, 128), f32)
            block = [jnp.concatenate([v, rest], axis=0) for v in block]
        for i in range(4):
            here = block[i]
            safe = jnp.where(here > 0.0, here, 1.0)
            above = block[i - 1] if i > 0 else jnp.where(sub == 0, 0.0, pltpu.roll(block[3], 1, 0))
            below = block[i + 1] if i < 3 else jnp.where(sub == 7, 0.0, pltpu.roll(block[0], 7, 0))
            side_c[0, i] = jnp.sqrt(above * here) / safe
            side_c[1, i] = jnp.sqrt(below * here) / safe
            side_c[2, i] = jnp.where(lane == 0, 0.0, jnp.sqrt(pltpu.roll(here, 1, 1) * here) / safe)
            side_c[3, i] = jnp.where(
                lane == 127, 0.0, jnp.sqrt(pltpu.roll(here, 127, 1) * here) / safe
            )
            for k in range(4 * i, 4 * i + 4):
                for m in range(4):
                    total = (
                        (side_c[0, i] if k % 4 == 0 else 1.0)
                        + (side_c[1, i] if k % 4 == 3 else 1.0)
                    ) + (
                        (side_c[2, i] if m == 0 else 1.0) + (side_c[3, i] if m == 3 else 1.0)
                    )
                    scaled = coarse_rate[m, pl.ds(k, 8, stride=16), :] * here
                    even[4 * k + m] = scaled
                    odd[4 * k + m] = scaled * total

        def one(p, carry):
            factor = steps_ref[lead_start + p].astype(f32) * (1.0 / (4.0 * CSUB))
            for v in range(64):
                weight_cd[p, v] = even[v] * factor
                weight_ce[p, v] = 1.0 - odd[v] * factor
            return carry

        lax.fori_loop(0, lead_size, one, 0)

    for t in range(n_sp):
        far = both(is_root, t != s)
        arrive(far, coarse_rate.at[:, pl.ds(16 * t, 16), :], s_crate.at[t])
        arrive(
            both(far, jnp.logical_not(close(t, 1))),
            tiles.at[pl.ds(8 * t + 8, 8), :],
            s_tile.at[t],
        )
    at(is_root, lead_setup)
    for t in range(n_sp):
        arrive(
            both(is_root, close(t, reach_here)), err_in.at[:, pl.ds(16 * t, 16), :], s_hop.at[t]
        )

    order = [k for k in range(2, 16, 2)] + [0] + [k for k in range(1, 16, 2)]

    def coarse_step(p, read, write, turned, turns, last):
        wrap_top = [jnp.where(sub == 0, 0.0, pltpu.roll(read[60 + m], 1, 0)) for m in range(4)]
        wrap_bottom = [jnp.where(sub == 7, 0.0, pltpu.roll(read[m], 7, 0)) for m in range(4)]
        for k in order:
            i = k // 4
            for m in (0, 3, 1, 2):
                v = 4 * k + m
                above = read[v - 4] if k > 0 else wrap_top[m]
                below = read[v + 4] if k < 15 else wrap_bottom[m]
                left = read[v - 1] if m > 0 else turned[0, k] * side_c[2, i]
                right = read[v + 1] if m < 3 else turned[1, k] * side_c[3, i]
                if k % 4 == 0:
                    above = above * side_c[0, i]
                if k % 4 == 3:
                    below = below * side_c[1, i]
                new = weight_ce[p, v] * read[v] + weight_cd[p, v] * (
                    (above + below) + (left + right)
                )
                if last:
                    where = (p, m, pl.ds(k, 8, stride=16), slice(None))
                    new = new + res_in[where]
                    err_out[where] = new
                write[v] = new
                if m == 3:
                    turns[0, k] = pltpu.roll(new, 1, 1)
                if m == 0:
                    turns[1, k] = pltpu.roll(new, 127, 1)

    def err_copy(p):
        return pltpu.make_async_remote_copy(
            src_ref=err_out.at[p, :, mine16, :],
            dst_ref=err_own,
            send_sem=s_errs.at[p],
            recv_sem=s_err,
            device_id=(lead_start + 1 + p, s),
            device_id_type=MESH,
        )

    def chain():
        for k in range(16):
            for m in range(4):
                even[4 * k + m] = err_in[m, pl.ds(k, 8, stride=16), :]
            even_turn[0, k] = pltpu.roll(even[4 * k + 3], 1, 1)
            even_turn[1, k] = pltpu.roll(even[4 * k], 127, 1)

        def stage(p, carry):
            reach = reach_of((lead_size - 1 - p) * CSUB)
            for t in range(n_sp):
                arrive(close(t, reach), res_in.at[p, :, pl.ds(16 * t, 16), :], s_res.at[p, t])
            for i in range(CSUB):
                if i % 2 == 0:
                    coarse_step(p, even, odd, even_turn, odd_turn, i == CSUB - 1)
                else:
                    coarse_step(p, odd, even, odd_turn, even_turn, False)
            at(p < lead_size - 1, lambda: err_copy(p).start())
            for v in range(64):
                even[v] = odd[v]
            for k in range(16):
                even_turn[0, k] = odd_turn[0, k]
                even_turn[1, k] = odd_turn[1, k]
            return carry

        lax.fori_loop(0, lead_size, stage, 0)

    at(is_root, chain)
    end = jnp.maximum(lead_size - 1, 0)
    for t in sorted(range(n_sp), key=lambda t: -abs(2 * t - n_sp + 1)):
        push(
            both(has_next, close(t, reach_next)),
            err_out.at[end, :, mine16, :],
            err_in.at[:, mine16, :],
            s_hop.at[s],
            next_root,
            t,
        )
    at(is_root, lambda: err_copy(end).start())

    relaxed = jnp.concatenate([hist_c[0, m, h_own, :] for m in range(8)], axis=1)
    nat_rel[...] = exact_dot(relaxed, back_w)

    def no_error():
        out_ref[0] = nat_rel[...]

    def with_error():
        errors = jnp.concatenate([err_own[m] for m in range(4)], axis=1)
        spread = exact_dot(errors, join_w)
        for c in range(8):
            columns = slice(128 * c, 128 * c + 128)
            nat_err[c, pl.ds(0, 16, stride=2), :] = spread[:, columns]
            nat_err[c, pl.ds(1, 16, stride=2), :] = spread[:, columns]
            out_ref[0, :, pl.ds(128 * c, 128)] = nat_rel[:, pl.ds(128 * c, 128)] + nat_err[c]

    arrive(j > 0, err_own, s_err)
    at(j == 0, no_error)
    at(j > 0, with_error)
    for cond, make in pending:
        at(cond, lambda make=make: make().wait_send())

    def drain():
        def one(p, carry):
            err_copy(p).wait_send()
            return carry

        lax.fori_loop(0, lead_size, one, 0)

    at(is_root, drain)


def advance(dims, *args):
    n_tm, n_sp, sizes, heads = dims
    most = max(sizes)
    f32 = jnp.float32
    bf16 = jnp.bfloat16
    vm = pltpu.VMEM
    sm = pltpu.SMEM
    dma = pltpu.SemaphoreType.DMA
    hist = (STEP_MOST // 2 + 1, 8, EXT + 2 * OFF, 128)
    hbm = pl.BlockSpec(memory_space=pltpu.HBM)
    return pl.pallas_call(
        functools.partial(kernel, dims),
        out_shape=jax.ShapeDtypeStruct((1, 32, 1024), f32),
        in_specs=[hbm] * 8,
        out_specs=pl.BlockSpec(memory_space=pltpu.VMEM),
        scratch_shapes=[
            sm(args[4].shape, f32),
            sm(args[5].shape, f32),
            sm(args[6].shape, jnp.int32),
            sm(args[7].shape, jnp.int32),
            vm((EXT, 1024), f32),
            vm((EXT, 1024), f32),
            vm((EXT, 1024), f32),
            vm((32, 1024), f32),
            vm(hist, f32),
            vm(hist, f32),
            vm(hist, f32),
            vm((8, EXT, 128), f32),
            vm((8, EXT, 128), f32),
            vm((8, EXT, 128), f32),
            vm((8, EXT, 128), f32),
            vm((BLOCKS, 5, 8, 128), f32),
            vm((8 * (n_sp + 2), 128), f32),
            vm((8, 32, 128), f32),
            vm((8, 32, 128), f32),
            vm((1024, 1024), bf16),
            vm((1024, 1024), bf16),
            vm((512, 1024), bf16),
            vm((4, 16, 128), f32),
            vm((4, 128, 128), f32),
            vm((most, 4, 128, 128), f32),
            vm((4, 128, 128), f32),
            vm((most, 64, 8, 128), f32),
            vm((most, 64, 8, 128), f32),
            vm((4, 4, 8, 128), f32),
            vm((64, 8, 128), f32),
            vm((64, 8, 128), f32),
            vm((2, 16, 8, 128), f32),
            vm((2, 16, 8, 128), f32),
            vm((most, 4, 128, 128), f32),
            vm((4, 16, 128), f32),
            vm((32, 1024), f32),
            vm((8, 32, 128), f32),
            dma((8,)),
            dma((72,)),
            dma((most,)),
            dma((2,)),
            dma((2,)),
            dma((2,)),
            dma((8,)),
            dma((8,)),
            dma((3,)),
            dma((most, 8)),
            dma((8,)),
            dma(()),
        ],
        compiler_params=pltpu.CompilerParams(
            collective_id=0, has_side_effects=True, vmem_limit_bytes=66846720
        ),
    )(*args)


def solution(mesh, sizes=GROUPS, heads=LEADS):
    placed = (
        P("tm", "space", None),
        P("space", None),
        P("space", None),
        P("space", None),
        P(),
        P(),
        P("space", None),
        P(),
    )
    dims = (mesh.shape["tm"], mesh.shape["space"], sizes, heads)
    return jax.shard_map(
        functools.partial(advance, dims),
        mesh=mesh,
        in_specs=placed,
        out_specs=P("tm", "space", None),
        check_vma=False,
    )
```

time: 979 us -> 68.5 us (0.07)
  the two profiles are of different devices: /device:TPU:136 before, /device:TPU:31 now
where the time goes in v2:
time: 68.5 us; the launch traced here: 68 us
  Pallas kernels  66.5 us (97%)
  local copies, waits for them, and re-layouts  1.57 us (2%)
    pallas_call x1, Pallas kernels, advance(): pl.pallas_call(functools.partial(kernel, dims), out_shape=jax.ShapeDtypeS...  66.5 us
    unnamed x1, local copies, waits for them, and re-layouts  1.57 us

profile of v2, /device:TPU:31, one launch (start us, length us, event | category | flops | bytes accessed | tf_op | source)
XLA Modules:
  0.0 68.0 jit_solution(14011353089607235443)
XLA Ops:
  0.0 66.5 %shard_map.82 = f32[1,32,1024]{2,1,0:T(8,128)} custom-call(f32[1,32,1024]{2,1,0:T(8,128)} %point_ref.1, f32[32,1024]{1,0:T(8,128)} %init_ref.1, f32[32,1024]{1,0:T(8,128)} %rate_ref.1, f32[32,1024]{1,0:T(8,128)} %src_ref.1, f32[512]{0:T(512)} %wave_hbm.1, f32[16]{0:T(128)} %table_hbm.1, s32[4,8]{1,0:T(4,128)} %class_hbm.1, s32[32]{0:T(128)} %steps_hbm.1), custom_call_target="tpu_custom_call" | custom-call | tf_op jit(solution)/shard_map/pallas_call | solution.py:666
  66.5 1.6 %copy.10 = f32[1,32,1024]{2,1,0:T(8,128)} copy(f32[1,32,1024]{2,1,0:T(8,128)} %shard_map.82) | data formatting | bytes 262144

commit v3 on v2

--- a/solution.py
+++ b/solution.py
@@ -15,7 +15,7 @@
 OFF = 8
 BLOCKS = EXT // 8
 PLAN = ((0, 2, 0, 10), (2, 6, 1, 9), (6, 10, 2, 8))
-GROUPS = (4, 13, 13)
+GROUPS = (4, 12, 14)
 LEADS = (6, 4, 12)
 
 
@@ -67,6 +67,7 @@
     err_own,
     nat_rel,
     nat_err,
+    s_ready,
     s_local,
     s_send,
     s_errs,
@@ -158,6 +159,9 @@
     def tell(cond, tm, sp):
         at(cond, lambda: signal(tm, sp))
 
+    tell(sender, root, s)
+    tell(j >= 2, pick(heads, out_group), s)
+    tell(has_next, next_root, s)
     signal(twin, s)
     for t in range(n_sp):
         beside = both(t != s, jnp.logical_or(is_root, close(t, 1)))
@@ -165,25 +169,7 @@
         tell(both(j > 0, close(t, 1)), j - 1, t)
         expect = expect + beside.astype(i32)
         expect = expect + both(j < n_tm - 1, close(t, 1)).astype(i32)
-        expect = expect + both(sender, close(t, reach_res)).astype(i32)
-        expect = expect + both(has_next, close(t, reach_next)).astype(i32)
-    tell(j >= 2, pick(heads, out_group), s)
-    expect = expect + jnp.where(is_root, lead_size, 0)
-
-    def greet_group():
-        before = jnp.where(lead == 0, 0, pick(heads, jnp.maximum(lead - 1, 0)))
-        for t in range(n_sp):
-            tell(close(t, reach_here), before, t)
-
-        def one(p, carry):
-            reach = reach_of((lead_size - 1 - p) * CSUB)
-            for t in range(n_sp):
-                tell(close(t, reach), lead_start + p, t)
-            return carry
-
-        lax.fori_loop(0, lead_size, one, 0)
-
-    at(is_root, greet_group)
+    expect = expect + jnp.where(is_root, 2 * lead_size + 1, 0)
 
     count = [0]
 
@@ -262,6 +248,22 @@
         push(both(core, down), ref.at[high, :], nat.at[above_rows, :], s_static.at[0], j, s + 1)
     push(up, point_ref.at[0, low, :], nat_point.at[below_rows, :], s_point.at[1], j, s - 1)
     push(down, point_ref.at[0, high, :], nat_point.at[above_rows, :], s_point.at[0], j, s + 1)
+
+    def answer():
+        def ready(which, tm):
+            pl.semaphore_signal(
+                s_ready.at[which], inc=1, device_id=(tm, s), device_id_type=MESH
+            )
+
+        def one(p, carry):
+            ready(0, lead_start + p)
+            return carry
+
+        lax.fori_loop(0, lead_size, one, 0)
+        at(lead == 0, lambda: ready(0, 0))
+        at(lead > 0, lambda: ready(1, pick(heads, jnp.maximum(lead - 1, 0))))
+
+    at(is_root, answer)
 
     def exact_dot(values, matrix):
         large = values.astype(bf16)
@@ -472,26 +474,6 @@
         both(follow, down), first.at[:, high, :], at_c.at[:, h_above, :], s_relax.at[0], j + 1, s + 1
     )
     push(follow, first, at_c.at[:, h_own, :], s_relax.at[1], j + 1, s)
-    arrive(j > 0, at_c.at[:, h_own, :], s_relax.at[1])
-    arrive(up, at_c.at[:, h_above, :], s_relax.at[0])
-    arrive(down, at_c.at[:, h_below, :], s_relax.at[2])
-    sweep(hist_c)
-
-    for m in range(8):
-        change[m] = state_after(hist_c, m, h_own) - first[m]
-    for m in range(4):
-        parts = []
-        for side in (0, 1):
-            part = change.at[2 * m + side]
-            parts.append(part[pl.ds(0, 16, stride=2), :] + part[pl.ds(1, 16, stride=2), :])
-        own_res[m] = 0.25 * (parts[0] + parts[1])
-    slot = jnp.clip(place, 0, max(sizes) - 1)
-    for t in range(n_sp):
-        cond = both(sender, close(t, reach_res))
-        push(both(cond, j > 0), own_res, res_in.at[slot, :, mine16, :], s_res.at[slot, s], root, t)
-        push(both(cond, j == 0), own_res, err_in.at[:, mine16, :], s_hop.at[s], root, t)
-    push(j == 0, own_res, err_own, s_err, j + 1, s)
-
     def lead_setup():
         block = [tiles[pl.ds(8 + i, n_sp, stride=8), :] for i in range(4)]
         if n_sp < 8:
@@ -538,31 +520,66 @@
             s_tile.at[t],
         )
     at(is_root, lead_setup)
+
+    arrive(j > 0, at_c.at[:, h_own, :], s_relax.at[1])
+    arrive(up, at_c.at[:, h_above, :], s_relax.at[0])
+    arrive(down, at_c.at[:, h_below, :], s_relax.at[2])
+    sweep(hist_c)
+
+    for m in range(8):
+        change[m] = state_after(hist_c, m, h_own) - first[m]
+    for m in range(4):
+        parts = []
+        for side in (0, 1):
+            part = change.at[2 * m + side]
+            parts.append(part[pl.ds(0, 16, stride=2), :] + part[pl.ds(1, 16, stride=2), :])
+        own_res[m] = 0.25 * (parts[0] + parts[1])
+    slot = jnp.clip(place, 0, max(sizes) - 1)
+    at(sender, lambda: pl.semaphore_wait(s_ready.at[0], 1))
+    for t in range(n_sp):
+        cond = both(sender, close(t, reach_res))
+        push(both(cond, j > 0), own_res, res_in.at[slot, :, mine16, :], s_res.at[slot, s], root, t)
+        push(both(cond, j == 0), own_res, err_in.at[:, mine16, :], s_hop.at[s], root, t)
+    push(j == 0, own_res, err_own, s_err, j + 1, s)
+
+    def residuals_in():
+        def one(p, carry):
+            reach = reach_of((lead_size - 1 - p) * CSUB)
+            for t in range(n_sp):
+                arrive(close(t, reach), res_in.at[p, :, pl.ds(16 * t, 16), :], s_res.at[p, t])
+            return carry
+
+        lax.fori_loop(0, lead_size, one, 0)
+
+    at(is_root, residuals_in)
     for t in range(n_sp):
         arrive(
             both(is_root, close(t, reach_here)), err_in.at[:, pl.ds(16 * t, 16), :], s_hop.at[t]
         )
 
-    order = [k for k in range(2, 16, 2)] + [0] + [k for k in range(1, 16, 2)]
-
     def coarse_step(p, read, write, turned, turns, last):
-        wrap_top = [jnp.where(sub == 0, 0.0, pltpu.roll(read[60 + m], 1, 0)) for m in range(4)]
-        wrap_bottom = [jnp.where(sub == 7, 0.0, pltpu.roll(read[m], 7, 0)) for m in range(4)]
-        for k in order:
+        def row(k):
+            if k == -1:
+                wrapped = [pltpu.roll(read[60 + m], 1, 0) for m in range(4)]
+                return [jnp.where(sub == 0, 0.0, v) for v in wrapped]
+            if k == 16:
+                wrapped = [pltpu.roll(read[m], 7, 0) for m in range(4)]
+                return [jnp.where(sub == 7, 0.0, v) for v in wrapped]
+            return [read[4 * k + m] for m in range(4)]
+
+        above, here = None, None
+        for k in range(16):
+            if k == 0:
+                above, here = row(-1), row(0)
+            below = row(k + 1)
             i = k // 4
             for m in (0, 3, 1, 2):
                 v = 4 * k + m
-                above = read[v - 4] if k > 0 else wrap_top[m]
-                below = read[v + 4] if k < 15 else wrap_bottom[m]
-                left = read[v - 1] if m > 0 else turned[0, k] * side_c[2, i]
-                right = read[v + 1] if m < 3 else turned[1, k] * side_c[3, i]
-                if k % 4 == 0:
-                    above = above * side_c[0, i]
-                if k % 4 == 3:
-                    below = below * side_c[1, i]
-                new = weight_ce[p, v] * read[v] + weight_cd[p, v] * (
-                    (above + below) + (left + right)
-                )
+                left = here[m - 1] if m > 0 else turned[0, k] * side_c[2, i]
+                right = here[m + 1] if m < 3 else turned[1, k] * side_c[3, i]
+                high = above[m] * side_c[0, i] if k % 4 == 0 else above[m]
+                deep = below[m] * side_c[1, i] if k % 4 == 3 else below[m]
+                new = weight_ce[p, v] * here[m] + weight_cd[p, v] * ((high + deep) + (left + right))
                 if last:
                     where = (p, m, pl.ds(k, 8, stride=16), slice(None))
                     new = new + res_in[where]
@@ -572,6 +589,7 @@
                     turns[0, k] = pltpu.roll(new, 1, 1)
                 if m == 0:
                     turns[1, k] = pltpu.roll(new, 127, 1)
+            above, here = here, below
 
     def err_copy(p):
         return pltpu.make_async_remote_copy(
@@ -590,27 +608,23 @@
             even_turn[0, k] = pltpu.roll(even[4 * k + 3], 1, 1)
             even_turn[1, k] = pltpu.roll(even[4 * k], 127, 1)
 
-        def stage(p, carry):
-            reach = reach_of((lead_size - 1 - p) * CSUB)
-            for t in range(n_sp):
-                arrive(close(t, reach), res_in.at[p, :, pl.ds(16 * t, 16), :], s_res.at[p, t])
-            for i in range(CSUB):
-                if i % 2 == 0:
-                    coarse_step(p, even, odd, even_turn, odd_turn, i == CSUB - 1)
-                else:
-                    coarse_step(p, odd, even, odd_turn, even_turn, False)
-            at(p < lead_size - 1, lambda: err_copy(p).start())
-            for v in range(64):
-                even[v] = odd[v]
-            for k in range(16):
-                even_turn[0, k] = odd_turn[0, k]
-                even_turn[1, k] = odd_turn[1, k]
+        def two_stages(h, carry):
+            p = 2 * h
+            bufs = ((even, even_turn), (odd, odd_turn))
+            for i in range(2 * CSUB):
+                (read, turned), (write, turns) = bufs[i % 2], bufs[(i + 1) % 2]
+                stage = p if i < CSUB else p + 1
+                coarse_step(stage, read, write, turned, turns, i % CSUB == CSUB - 1)
+                if i == CSUB - 1:
+                    err_copy(p).start()
+            at(p + 1 < lead_size - 1, lambda: err_copy(p + 1).start())
             return carry
 
-        lax.fori_loop(0, lead_size, stage, 0)
+        lax.fori_loop(0, lead_size // 2, two_stages, 0)
 
     at(is_root, chain)
     end = jnp.maximum(lead_size - 1, 0)
+    at(has_next, lambda: pl.semaphore_wait(s_ready.at[1], 1))
     for t in sorted(range(n_sp), key=lambda t: -abs(2 * t - n_sp + 1)):
         push(
             both(has_next, close(t, reach_next)),
@@ -706,6 +720,7 @@
             vm((4, 16, 128), f32),
             vm((32, 1024), f32),
             vm((8, 32, 128), f32),
+            pltpu.SemaphoreType.REGULAR((2,)),
             dma((8,)),
             dma((72,)),
             dma((most,)),

time: 68.5 us -> 65.1 us (0.950)
  Pallas kernels: 66.5 us -> 63.4 us
    pallas_call x1, Pallas kernels: 66.5 us -> 63.4 us  [advance(): pl.pallas_call(functools.partial(kernel, dims), out_shape=jax.ShapeDtypeS...]
where the time goes in v3:
time: 65.1 us; the launch traced here: 65 us
  Pallas kernels  63.4 us (97%)
  local copies, waits for them, and re-layouts  1.57 us (2%)
    pallas_call x1, Pallas kernels, advance(): pl.pallas_call(functools.partial(kernel, dims), out_shape=jax.ShapeDtypeS...  63.4 us
    unnamed x1, local copies, waits for them, and re-layouts  1.57 us

profile of v3, /device:TPU:31, one launch (start us, length us, event | category | flops | bytes accessed | tf_op | source)
XLA Modules:
  0.0 65.0 jit_solution(18310151481190087044)
XLA Ops:
  0.0 63.4 %shard_map.82 = f32[1,32,1024]{2,1,0:T(8,128)} custom-call(f32[1,32,1024]{2,1,0:T(8,128)} %point_ref.1, f32[32,1024]{1,0:T(8,128)} %init_ref.1, f32[32,1024]{1,0:T(8,128)} %rate_ref.1, f32[32,1024]{1,0:T(8,128)} %src_ref.1, f32[512]{0:T(512)} %wave_hbm.1, f32[16]{0:T(128)} %table_hbm.1, s32[4,8]{1,0:T(4,128)} %class_hbm.1, s32[32]{0:T(128)} %steps_hbm.1), custom_call_target="tpu_custom_call" | custom-call | tf_op jit(solution)/shard_map/pallas_call | solution.py:680
  63.4 1.6 %copy.10 = f32[1,32,1024]{2,1,0:T(8,128)} copy(f32[1,32,1024]{2,1,0:T(8,128)} %shard_map.82) | data formatting | bytes 262144

commit v4 on v3

--- a/solution.py
+++ b/solution.py
@@ -363,8 +363,6 @@
         join_w[pl.ds(pl.multiple_of(64 * i, 64), 64), :] = jnp.where(hit, 1.0, 0.0).astype(bf16)
         return carry
 
-    lax.fori_loop(0, 16, fill_back, 0)
-    lax.fori_loop(0, 8, fill_join, 0)
 
     loads[6].wait()
     loads[7].wait()
@@ -411,11 +409,13 @@
                 weight_e[m, rows, :] = 1.0 - scaled * total
 
     weigh(range(3, 7))
+    at(first_core, lambda: halos_to_parts(nat_rate, put_in(rows_rate)))
+    at(second_core, lambda: halos_to_parts(nat_src, put_in(rows_src)))
     for core, nat in ((first_core, nat_src), (second_core, nat_rate)):
         for side, where, sem in ((up, above_rows, 0), (down, below_rows, 1)):
             arrive(both(core, side), nat.at[where, :], s_share.at[sem])
-    halos_to_parts(nat_rate, put_in(rows_rate))
-    halos_to_parts(nat_src, put_in(rows_src))
+    at(second_core, lambda: halos_to_parts(nat_rate, put_in(rows_rate)))
+    at(first_core, lambda: halos_to_parts(nat_src, put_in(rows_src)))
     weigh((0, 1, 2, 7, 8, 9))
     arrive(up, nat_point.at[above_rows, :], s_point.at[0])
     arrive(down, nat_point.at[below_rows, :], s_point.at[1])
@@ -521,6 +521,8 @@
         )
     at(is_root, lead_setup)
 
+    lax.fori_loop(0, 16, fill_back, 0)
+    lax.fori_loop(0, 8, fill_join, 0)
     arrive(j > 0, at_c.at[:, h_own, :], s_relax.at[1])
     arrive(up, at_c.at[:, h_above, :], s_relax.at[0])
     arrive(down, at_c.at[:, h_below, :], s_relax.at[2])

time: 65.1 us -> 65.1 us (level)
  no operation moved by 1% of the time
where the time goes in v4:
time: 65.1 us; the launch traced here: 65 us
  Pallas kernels  63.4 us (97%)
  local copies, waits for them, and re-layouts  1.57 us (2%)
    pallas_call x1, Pallas kernels, advance(): pl.pallas_call(functools.partial(kernel, dims), out_shape=jax.ShapeDtypeS...  63.4 us
    unnamed x1, local copies, waits for them, and re-layouts  1.57 us

profile of v4, /device:TPU:31, one launch (start us, length us, event | category | flops | bytes accessed | tf_op | source)
XLA Modules:
  0.0 65.0 jit_solution(14806745813146900582)
XLA Ops:
  0.0 63.4 %shard_map.82 = f32[1,32,1024]{2,1,0:T(8,128)} custom-call(f32[1,32,1024]{2,1,0:T(8,128)} %point_ref.1, f32[32,1024]{1,0:T(8,128)} %init_ref.1, f32[32,1024]{1,0:T(8,128)} %rate_ref.1, f32[32,1024]{1,0:T(8,128)} %src_ref.1, f32[512]{0:T(512)} %wave_hbm.1, f32[16]{0:T(128)} %table_hbm.1, s32[4,8]{1,0:T(4,128)} %class_hbm.1, s32[32]{0:T(128)} %steps_hbm.1), custom_call_target="tpu_custom_call" | custom-call | tf_op jit(solution)/shard_map/pallas_call | solution.py:682
  63.4 1.6 %copy.10 = f32[1,32,1024]{2,1,0:T(8,128)} copy(f32[1,32,1024]{2,1,0:T(8,128)} %shard_map.82) | data formatting | bytes 262144
